TPU v7x, 128 devices: a whole 4x4x4 slice. The times are simulated.
128 devices in a mesh: tp: 4 (over y), ad: 32 (over x, z, core).
Axes of the slice: x: 4, y: 4, z: 4, core: 2. Of those that a mesh axis runs over, the one named last changes fastest.
Arguments:
- queries: bfloat16 [8192, 4096], P('ad', 'tp'), may hold values from -300 to 300
- key_cache: bfloat16 [8192, 128, 512], P('ad', None, 'tp'), may hold values from -4 to 4
- value_cache: bfloat16 [8192, 128, 512], P('ad', None, 'tp'), may hold values from -6 to 6
- new_key: bfloat16 [8192, 512], P('ad', 'tp'), may hold values from -6 to 6
- new_value: bfloat16 [8192, 512], P('ad', 'tp'), may hold values from -6 to 6
- lengths: int32 [8192], P('ad'), may hold values from 2 to 128, as said below
- out_weight: bfloat16 [4096, 8192], P('tp'), may hold values from -0.09375 to 0.09375
- shrink_weight: bfloat16 [4096, 16384], P('tp', 'ad'), may hold values from -0.09375 to 0.09375
- expand_weight: bfloat16 [16384, 8192], P('ad', 'tp'), may hold values from -0.75 to 0.75
- adapter_id: int32 [8192], P('ad'), may hold values from 0 to 255, as said below
- adapter_slot: int32 [256], replicated, may hold values from 0 to 255, as said below
Outputs:
- projected: bfloat16 [8192, 8192], P('ad', 'tp')
Inputs may be any that keep to these rules, and one draw needn't show every extreme that they name: `adapter_id`: rows are grouped by adapter within the rows of one device. Owner of adapter a is adapter_slot[a] // 8. The rows of one device name at most 16 rows for each owner, and every device names exactly 16 rows for one common owner drawn from the seed. `adapter_slot`: each value once. `lengths`: some row of every device has 128.
All inputs are finite; a program needn't handle non-finite values.
Results may differ from a plain program's by a relative error of at most 0.011.
Values may be sent and summed in bfloat16 or wider, within the bound.
A program may use at most 128 MiB of HBM per device.

v0:
```python
import math
import jax
import jax.numpy as jnp
from jax import lax
from jax.sharding import PartitionSpec as P

HEADS = 32
KV_HEADS = 4
HEAD_DIM = 128
RANK = 64


def attend(queries, key_cache, value_cache, new_key, new_value, lengths):
    row_count = queries.shape[0]
    slots = key_cache.shape[1]
    kv_local = key_cache.shape[2] // HEAD_DIM
    group = HEADS // KV_HEADS
    scale = 1.0 / math.sqrt(HEAD_DIM)
    query_four = queries.reshape(row_count, kv_local, group, HEAD_DIM)
    key_four = key_cache.reshape(row_count, slots, kv_local, HEAD_DIM)
    value_four = value_cache.reshape(row_count, slots, kv_local, HEAD_DIM)
    fresh_key = new_key.reshape(row_count, kv_local, HEAD_DIM)
    fresh_value = new_value.reshape(row_count, kv_local, HEAD_DIM).astype(jnp.float32)
    scores = (
        jnp.einsum("rkgd,rckd->rkgc", query_four, key_four, preferred_element_type=jnp.float32)
        * scale
    )
    own = (
        jnp.einsum("rkgd,rkd->rkg", query_four, fresh_key, preferred_element_type=jnp.float32)
        * scale
    )
    valid = jnp.arange(slots)[None, :] < lengths[:, None]
    valid = valid[:, None, None, :]
    scores = jnp.where(valid, scores, -jnp.inf)
    top = jnp.maximum(jnp.max(scores, axis=-1), own)
    expo = jnp.where(valid, jnp.exp(scores - top[..., None]), 0.0)
    own_expo = jnp.exp(own - top)
    total = jnp.sum(expo, axis=-1) + own_expo
    probs = (expo / total[..., None]).astype(jnp.bfloat16)
    own_prob = (own_expo / total).astype(jnp.bfloat16)
    mixed = jnp.einsum("rkgc,rckd->rkgd", probs, value_four, preferred_element_type=jnp.float32)
    mixed = mixed + own_prob.astype(jnp.float32)[..., None] * fresh_value[:, :, None, :]
    return mixed.reshape(row_count, kv_local * group * HEAD_DIM).astype(jnp.bfloat16)


def adapt(arrived, local_ids, shrink_weight, expand_weight, reduce_heads):
    owner_count, slot_count, width = arrived.shape
    flat_rows = arrived.reshape(owner_count * slot_count, width)
    flat_ids = local_ids.reshape(owner_count * slot_count)
    held = shrink_weight.shape[1] // RANK
    full_shrink = jnp.dot(flat_rows, shrink_weight, preferred_element_type=jnp.float32)
    which = jnp.arange(held * RANK, dtype=jnp.int32) // RANK
    picks = flat_ids[:, None] == which[None, :]
    partial_value = jnp.where(picks, full_shrink, 0.0).reshape(-1, held, RANK).sum(axis=1)
    shrunk = reduce_heads(partial_value).astype(jnp.bfloat16)
    spread = jnp.where(picks, jnp.tile(shrunk, (1, held)), jnp.zeros((), jnp.bfloat16))
    widened = jnp.dot(spread, expand_weight, preferred_element_type=jnp.float32).astype(
        jnp.bfloat16
    )
    return widened.reshape(owner_count, slot_count, widened.shape[1])


def shards(
    queries,
    key_cache,
    value_cache,
    new_key,
    new_value,
    lengths,
    out_weight,
    shrink_weight,
    expand_weight,
    adapter_id,
    adapter_slot,
):
    attended = attend(queries, key_cache, value_cache, new_key, new_value, lengths)
    row_count, width = attended.shape
    held = shrink_weight.shape[1] // RANK
    catalog = jnp.arange(adapter_slot.shape[0], dtype=jnp.int32)
    slot = jnp.sum(
        jnp.where(adapter_id[:, None] == catalog[None, :], adapter_slot[None, :], 0), axis=1
    )
    owner = slot // held
    local_index = slot % held
    owner_count = lax.axis_size("ad")
    capacity = 2 * row_count // owner_count
    owner_hits = (owner[:, None] == jnp.arange(owner_count, dtype=jnp.int32)[None, :]).astype(
        jnp.int32
    )
    earlier = jnp.cumsum(owner_hits, axis=0) - owner_hits
    place = owner * capacity + jnp.sum(earlier * owner_hits, axis=1)
    select = place[None, :] == jnp.arange(owner_count * capacity, dtype=jnp.int32)[:, None]
    select_matrix = select.astype(jnp.bfloat16)
    packed = jnp.dot(select_matrix, attended, preferred_element_type=jnp.float32).astype(
        jnp.bfloat16
    )
    packed = packed.reshape(owner_count, capacity, width)
    slot_index = jnp.sum(jnp.where(select, local_index[None, :], 0), axis=1).reshape(
        owner_count, capacity
    )
    arrived, local_ids = (
        lax.all_to_all(packed, "ad", split_axis=0, concat_axis=0, tiled=True),
        lax.all_to_all(slot_index, "ad", split_axis=0, concat_axis=0, tiled=True),
    )
    widened = adapt(
        arrived,
        local_ids,
        shrink_weight,
        expand_weight,
        lambda partial_value: lax.psum(partial_value, "tp"),
    )
    returned = lax.all_to_all(widened, "ad", split_axis=0, concat_axis=0, tiled=True)
    returned = returned.reshape(owner_count * capacity, returned.shape[2])
    adapted = jnp.dot(select_matrix.T, returned, preferred_element_type=jnp.float32)
    partial_base = jnp.dot(attended, out_weight, preferred_element_type=jnp.float32)
    base = lax.psum_scatter(partial_base, "tp", scatter_dimension=1, tiled=True)
    return (base + adapted).astype(jnp.bfloat16)


def solution(mesh):
    in_specs = (
        P("ad", "tp"),
        P("ad", None, "tp"),
        P("ad", None, "tp"),
        P("ad", "tp"),
        P("ad", "tp"),
        P("ad"),
        P("tp", None),
        P("tp", "ad"),
        P("ad", "tp"),
        P("ad"),
        P(),
    )
    out_specs = P("ad", "tp")
    return jax.shard_map(shards, mesh=mesh, in_specs=in_specs, out_specs=out_specs, check_vma=False)
```

profile of v0, /device:TPU:1, one launch (start us, length us, event | category | flops | bytes accessed | tf_op | source)
XLA Modules:
  0.0 150.0 jit_solution(10672959812957457667)
XLA Ops:
  6.5 1.3 copy.32
  7.8 0.8 iota_compare_fusion.4
  8.7 1.5 convert_element_type.45
  10.1 6.9 %fusion.32 = (f32[256,8]{1,0:T(8,128)S(1)}, f32[256,8,128]{2,1,0:T(8,128)S(1)}) fusion(bf16[256,8,128]{2,1,0:T(8,128)(2,1)S(1)} %bitcast.71, bf16[256,128,128]{2,1,0:T(8,128)(2,1)} %param.12, pred[256,128]{1,0:T(8,128)(4,1)S(1)} %iota_compare_fusion.4), kind=kOutput, calls=%fused_computation.71 | convolution fusion | flops 67893248 | bytes 10002432 | tf_op jit(solution)/shard_map/rkgd,rckd->rkgc/dot_general | solution.py:25
  17.1 1.5 fusion.18
  18.7 0.1 copy.23
  18.8 0.7 fusion.3
  19.6 0.1 copy.26
  19.8 0.8 copy.25
  20.6 5.7 %fusion.2 = bf16[256,8,128]{2,1,0:T(8,128)(2,1)S(1)} fusion(bf16[256,128,128]{2,1,0:T(8,128)(2,1)} %param.13, f32[256,8,128]{2,1,0:T(8,128)S(1)} %get-tuple-element.10, f32[256,128]{1,0:T(8,128)} %convert_element_type.45, f32[256,8]{1,0:T(8,128)S(1)} %copy.26, f32[256,8]{1,0:T(8,128)} %copy.25, f32[256,8]{1,0:T(8,128)S(1)} %copy.23, ...), kind=kOutput, calls=%fused_computation.9 | convolution fusion | flops 68943872 | bytes 10149888 | tf_op jit(solution)/shard_map/rkgc,rckd->rkgd/dot_general | solution.py:41
  26.3 0.8 copy-done.1
  27.1 12.5 %fusion.5 = f32[256,8192]{1,0:T(8,128)} fusion(bf16[1024,8192]{1,0:T(8,128)(2,1)} %param.17, bf16[32,8,8,128]{3,2,1,0:T(8,128)(2,1)S(1)} %bitcast.69), kind=kOutput, calls=%fused_computation.14 | convolution fusion | flops 4294967296 | bytes 25690112 | tf_op jit(solution)/shard_map/dot_general | solution.py:115
  39.6 0.6 copy-done.4
  40.2 0.2 select_reduce_fusion.1
  40.4 0.6 reduce-window.6
  41.0 0.2 slice_reduce_fusion
  41.3 0.1 fusion.22
  41.4 0.2 select_reduce_fusion
  41.5 0.7 all_to_all.12
  42.2 9.4 %all-to-all-start = ((s32[32,1,16]{2,1,0:T(1,128)}), s32[32,1,16]{2,1,0:T(1,128)S(1)}, u32[]{:S(2)}, u32[]{:S(2)}) async-start(s32[32,1,16]{2,1,0:T(1,128)} %bitcast.4), calls=%async_computation.1 | async-start | bytes 32768 | tf_op jit(solution)/shard_map/all_to_all | solution.py:103
  51.7 1.4 convolution_convert_fusion.1
  53.1 5.5 %all-to-all-done = s32[32,1,16]{2,1,0:T(1,128)S(1)} async-done(((s32[32,1,16]{2,1,0:T(1,128)}), s32[32,1,16]{2,1,0:T(1,128)S(1)}, u32[]{:S(2)}, u32[]{:S(2)}) %all-to-all-start) | async-done | bytes 2080 | tf_op jit(solution)/shard_map/all_to_all | solution.py:103
  58.6 4.2 %all-to-all-start.1 = ((bf16[32,16,1024]{2,1,0:T(8,128)(2,1)}), bf16[32,16,1024]{2,1,0:T(8,128)(2,1)S(1)}, u32[]{:S(2)}, u32[]{:S(2)}) async-start(bf16[32,16,1024]{2,1,0:T(8,128)(2,1)} %bitcast.5), calls=%async_computation.2 | async-start | bytes 2097152 | tf_op jit(solution)/shard_map/all_to_all | solution.py:102
  62.9 0.6 broadcast.200
  63.4 0.7 reduce.9
  64.2 15.6 %all-to-all-done.1 = bf16[32,16,1024]{2,1,0:T(8,128)(2,1)S(1)} async-done(((bf16[32,16,1024]{2,1,0:T(8,128)(2,1)}), bf16[32,16,1024]{2,1,0:T(8,128)(2,1)S(1)}, u32[]{:S(2)}, u32[]{:S(2)}) %all-to-all-start.1) | async-done | bytes 1048608 | tf_op jit(solution)/shard_map/all_to_all | solution.py:102
  79.9 3.0 %convolution_select_fusion = f32[512,512]{0,1:T(8,128)} fusion(bf16[512,1024]{1,0:T(8,128)(2,1)S(1)} %bitcast.74, bf16[1024,512]{1,0:T(8,128)(2,1)} %param.18, s32[512]{0:T(512)S(1)} %eq.76, s32[512]{0:T(512)S(1)} %add_select_fusion), kind=kOutput, calls=%fused_computation.7 | convolution fusion | flops 537395200 | bytes 3149824 | tf_op jit(solution)/shard_map/dot_general | solution.py:51
  82.8 1.3 reduce_sum.52
  84.1 19.2 %all-reduce.1 = bf16[512,64]{0,1:T(8,128)(2,1)S(1)} all-reduce(f32[512,64]{0,1:T(8,128)S(1)} %reduce_sum.52), channel_id=1, replica_groups=mesh['tp'=4,'ad'=32] {'tp'}, use_global_device_ids=true, to_apply=%region_9.10 | all-reduce | flops 32768 | bytes 196608 | tf_op jit(solution)/shard_map/psum | solution.py:110
  103.3 1.4 convolution_convert_fusion
  104.7 34.4 %all_to_all.19 = bf16[32,16,2048]{2,1,0:T(8,128)(2,1)} all-to-all(bf16[32,16,2048]{2,1,0:T(8,128)(2,1)S(1)} %bitcast.73), channel_id=1, replica_groups=mesh['tp'=4,'ad'=32] {'ad'}, dimensions={0} | all-to-all | bytes 4194304 | tf_op jit(solution)/shard_map/all_to_all | solution.py:112
  139.2 4.0 %fusion = bf16[256,2048]{1,0:T(8,128)(2,1)} fusion(f32[256,2048]{1,0:T(8,128)} %reduce-scatter.2.cloned.1.call-done, bf16[512,2048]{1,0:T(8,128)(2,1)} %bitcast.68, s32[256]{0:T(256)S(1)} %multiply_add_fusion), kind=kOutput, calls=%fused_computation.2 | convolution fusion | flops 538050560 | bytes 5243904 | tf_op jit(solution)/shard_map/dot_general | solution.py:114
  (29 shorter events, 0.5 us)
Async XLA Ops:
  6.5 96.8 %copy-start = (bf16[512,2048]{1,0:T(8,128)(2,1)S(1)}, bf16[512,2048]{1,0:T(8,128)(2,1)}, u32[]{:S(2)}) copy-start(bf16[512,2048]{1,0:T(8,128)(2,1)} %param.19) | copy-start | bytes 6291460
  6.5 132.6 %reduce-scatter.2.cloned.1.call-start = ((), (), s32[]{:S(2)}) async-start(), calls=%async_computation.4 | async-start | bytes 10485760 | tf_op jit(solution)/shard_map/reduce_scatter | solution.py:116
  7.8 9.2 %copy-start.3 = (bf16[32,8,8,128]{3,2,1,0:T(8,128)(2,1)}, bf16[32,8,8,128]{3,2,1,0:T(8,128)(2,1)S(1)}, u32[]{:S(2)}) copy-start(bf16[32,8,8,128]{3,2,1,0:T(8,128)(2,1)S(1)} %copy.32) | copy-start | bytes 1572868
  10.1 7.0 %copy-start.6 = (bf16[256,128]{1,0:T(8,128)(2,1)S(1)}, bf16[256,128]{1,0:T(8,128)(2,1)}, u32[]{:S(2)}) copy-start(bf16[256,128]{1,0:T(8,128)(2,1)} %param.14) | copy-start | bytes 196612
  26.3 0.8 copy-start.1
  39.5 0.7 copy-start.4
  39.5 0.7 copy-start.5
  39.5 12.1 %copy-start.2 = (bf16[256,8,128]{2,1,0:T(8,128)(2,1)S(1)}, bf16[256,8,128]{2,1,0:T(8,128)(2,1)}, u32[]{:S(2)}) copy-start(bf16[256,8,128]{2,1,0:T(8,128)(2,1)} %copy-done.1) | copy-start | bytes 1572868
  42.2 16.4 %all-to-all-start = ((s32[32,1,16]{2,1,0:T(1,128)}), s32[32,1,16]{2,1,0:T(1,128)S(1)}, u32[]{:S(2)}, u32[]{:S(2)}) async-start(s32[32,1,16]{2,1,0:T(1,128)} %bitcast.4), calls=%async_computation.1 | async-start | bytes 32768 | tf_op jit(solution)/shard_map/all_to_all | solution.py:103
  58.6 21.2 %all-to-all-start.1 = ((bf16[32,16,1024]{2,1,0:T(8,128)(2,1)}), bf16[32,16,1024]{2,1,0:T(8,128)(2,1)S(1)}, u32[]{:S(2)}, u32[]{:S(2)}) async-start(bf16[32,16,1024]{2,1,0:T(8,128)(2,1)} %bitcast.5), calls=%async_computation.2 | async-start | bytes 2097152 | tf_op jit(solution)/shard_map/all_to_all | solution.py:102
Sparse Core Ops, SparseCore 0:
  39.7 86.2 reduce-scatter.1
where the time goes:
time: 151 us; the launch traced here: 150 us
  blocking collectives  53.6 us (35%)
  matrix products  36.3 us (24%)
  waiting for transfers between devices  21.2 us (14%)
  starting transfers between devices  13.7 us (9%)
  between operations  13.6 us (9%)
  other arithmetic  6.13 us (4%)
  local copies, waits for them, and re-layouts  5.59 us (4%)
    all_to_all x1, blocking collectives, shards(): lax.all_to_all(widened, 'ad', split_axis=0, concat_axis=0, tiled=True)  34.4 us
    psum x1, blocking collectives, shards(): lax.psum(partial_value, 'tp')  19.2 us
    all_to_all x1, waiting for transfers between devices, shards(): lax.all_to_all(packed, 'ad', split_axis=0, concat_axis=0, tiled=True)  15.6 us
    dot_general x1, matrix products, shards(): jnp.dot(attended, out_weight, preferred_element_type=jnp.float32)  12.5 us
    all_to_all x1, starting transfers between devices, shards(): lax.all_to_all(slot_index, 'ad', split_axis=0, concat_axis=0, tiled=True)  9.43 us
    dot_general x1, matrix products, attend(): jnp.einsum('rkgd,rckd->rkgc', query_four, key_four, preferred_element_typ...  6.92 us
    dot_general x1, matrix products, attend(): jnp.einsum('rkgc,rckd->rkgd', probs, value_four, preferred_element_type=j...  5.72 us
    all_to_all x1, waiting for transfers between devices, shards(): lax.all_to_all(slot_index, 'ad', split_axis=0, concat_axis=0, tiled=True)  5.52 us
  transfers between devices with their start and end apart: 3, of which 2 were waited for; matrix products, arithmetic and copies ran while one was open for 6% of the time, Pallas kernels for 0%

commit v1 on v0

--- a/solution.py
+++ b/solution.py
@@ -107,7 +107,7 @@
         local_ids,
         shrink_weight,
         expand_weight,
-        lambda partial_value: lax.psum(partial_value, "tp"),
+        lambda partial_value: jnp.sum(lax.all_gather(partial_value, "tp"), axis=0),
     )
     returned = lax.all_to_all(widened, "ad", split_axis=0, concat_axis=0, tiled=True)
     returned = returned.reshape(owner_count * capacity, returned.shape[2])

time: 151 us -> 146 us (0.967)
  blocking collectives: 53.6 us -> 48.2 us
    psum x1 -> x0, blocking collectives: 19.2 us -> none  [shards(): lax.psum(partial_value, 'tp')]
    all_gather x0 -> x1, blocking collectives: none -> 14.9 us  [shards(): lax.all_gather(partial_value, 'tp')]
  transfers between devices with their start and end apart: 3 -> 3, of which waited for: 2 -> 2; matrix products, arithmetic and copies ran while one was open for 6% -> 7% of each run, Pallas kernels for 0% -> 0%
where the time goes in v1:
time: 146 us; the launch traced here: 145 us
  blocking collectives  48.2 us (33%)
  matrix products  36.3 us (25%)
  waiting for transfers between devices  21.1 us (14%)
  starting transfers between devices  13.7 us (9%)
  between operations  13.6 us (9%)
  other arithmetic  6.44 us (4%)
  local copies, waits for them, and re-layouts  5.94 us (4%)
    all_to_all x1, blocking collectives, shards(): lax.all_to_all(widened, 'ad', split_axis=0, concat_axis=0, tiled=True)  33.3 us
    all_to_all x1, waiting for transfers between devices, shards(): lax.all_to_all(packed, 'ad', split_axis=0, concat_axis=0, tiled=True)  15.6 us
    all_gather x1, blocking collectives, shards(): lax.all_gather(partial_value, 'tp')  14.9 us
    dot_general x1, matrix products, shards(): jnp.dot(attended, out_weight, preferred_element_type=jnp.float32)  12.5 us
    all_to_all x1, starting transfers between devices, shards(): lax.all_to_all(slot_index, 'ad', split_axis=0, concat_axis=0, tiled=True)  9.43 us
    dot_general x1, matrix products, attend(): jnp.einsum('rkgd,rckd->rkgc', query_four, key_four, preferred_element_typ...  6.92 us
    dot_general x1, matrix products, attend(): jnp.einsum('rkgc,rckd->rkgd', probs, value_four, preferred_element_type=j...  5.72 us
    all_to_all x1, waiting for transfers between devices, shards(): lax.all_to_all(slot_index, 'ad', split_axis=0, concat_axis=0, tiled=True)  5.51 us
  transfers between devices with their start and end apart: 3, of which 2 were waited for; matrix products, arithmetic and copies ran while one was open for 7% of the time, Pallas kernels for 0%

profile of v1, /device:TPU:1, one launch (start us, length us, event | category | flops | bytes accessed | tf_op | source)
XLA Modules:
  0.0 145.3 jit_solution(450671847596070207)
XLA Ops:
  6.5 1.3 copy.32
  7.8 0.8 iota_compare_fusion.4
  8.7 1.5 %convert_element_type.49 = f32[256,128]{1,0:T(8,128)} convert(bf16[256,128]{1,0:T(8,128)(2,1)} %param.15) | non-fusion elementwise | flops 32768 | bytes 196608 | tf_op jit(solution)/shard_map/convert_element_type | solution.py:23
  10.1 6.9 %fusion.32 = (f32[256,8]{1,0:T(8,128)S(1)}, f32[256,8,128]{2,1,0:T(8,128)S(1)}) fusion(bf16[256,8,128]{2,1,0:T(8,128)(2,1)S(1)} %bitcast.73, bf16[256,128,128]{2,1,0:T(8,128)(2,1)} %param.12, pred[256,128]{1,0:T(8,128)(4,1)S(1)} %iota_compare_fusion.4), kind=kOutput, calls=%fused_computation.71 | convolution fusion | flops 67893248 | bytes 10002432 | tf_op jit(solution)/shard_map/rkgd,rckd->rkgc/dot_general | solution.py:25
  17.1 1.5 %fusion.18 = f32[256,1,8]{2,1,0:T(1,128)S(1)} fusion(bf16[256,8,128]{2,1,0:T(8,128)(2,1)} %bitcast.74, bf16[256,128,1]{1,0,2:T(8,128)(2,1)S(1)} %bitcast.80), kind=kOutput, calls=%fused_computation.32 | convolution fusion | flops 524288 | bytes 598016 | tf_op jit(solution)/shard_map/rkgd,rkd->rkg/dot_general | solution.py:29
  18.7 0.1 copy.23
  18.8 0.7 fusion.3
  19.8 0.8 copy.25
  20.6 5.7 %fusion.2 = bf16[256,8,128]{2,1,0:T(8,128)(2,1)S(1)} fusion(bf16[256,128,128]{2,1,0:T(8,128)(2,1)} %param.13, f32[256,8,128]{2,1,0:T(8,128)S(1)} %get-tuple-element.10, f32[256,128]{1,0:T(8,128)} %convert_element_type.49, f32[256,8]{1,0:T(8,128)S(1)} %copy.26, f32[256,8]{1,0:T(8,128)} %copy.25, f32[256,8]{1,0:T(8,128)S(1)} %copy.23, ...), kind=kOutput, calls=%fused_computation.9 | convolution fusion | flops 68943872 | bytes 10149888 | tf_op jit(solution)/shard_map/rkgc,rckd->rkgd/dot_general | solution.py:41
  26.3 0.8 copy-done.1
  27.1 12.5 %fusion.5 = f32[256,8192]{1,0:T(8,128)} fusion(bf16[1024,8192]{1,0:T(8,128)(2,1)} %param.17, bf16[32,8,8,128]{3,2,1,0:T(8,128)(2,1)S(1)} %bitcast.71), kind=kOutput, calls=%fused_computation.14 | convolution fusion | flops 4294967296 | bytes 25690112 | tf_op jit(solution)/shard_map/dot_general | solution.py:115
  39.6 0.6 copy-done.4
  40.2 0.2 select_reduce_fusion.1
  40.4 0.6 reduce-window.6
  41.0 0.2 slice_reduce_fusion
  41.4 0.2 select_reduce_fusion
  41.5 0.7 all_to_all.12
  42.2 9.4 %all-to-all-start = ((s32[32,1,16]{2,1,0:T(1,128)}), s32[32,1,16]{2,1,0:T(1,128)S(1)}, u32[]{:S(2)}, u32[]{:S(2)}) async-start(s32[32,1,16]{2,1,0:T(1,128)} %bitcast.4), calls=%async_computation.1 | async-start | bytes 32768 | tf_op jit(solution)/shard_map/all_to_all | solution.py:103
  51.7 1.4 convolution_convert_fusion.1
  53.1 5.5 %all-to-all-done = s32[32,1,16]{2,1,0:T(1,128)S(1)} async-done(((s32[32,1,16]{2,1,0:T(1,128)}), s32[32,1,16]{2,1,0:T(1,128)S(1)}, u32[]{:S(2)}, u32[]{:S(2)}) %all-to-all-start) | async-done | bytes 2080 | tf_op jit(solution)/shard_map/all_to_all | solution.py:103
  58.6 4.2 %all-to-all-start.1 = ((bf16[32,16,1024]{2,1,0:T(8,128)(2,1)}), bf16[32,16,1024]{2,1,0:T(8,128)(2,1)S(1)}, u32[]{:S(2)}, u32[]{:S(2)}) async-start(bf16[32,16,1024]{2,1,0:T(8,128)(2,1)} %bitcast.5), calls=%async_computation.2 | async-start | bytes 2097152 | tf_op jit(solution)/shard_map/all_to_all | solution.py:102
  62.9 0.6 broadcast.200
  63.4 0.7 reduce.9
  64.2 15.6 %all-to-all-done.1 = bf16[32,16,1024]{2,1,0:T(8,128)(2,1)S(1)} async-done(((bf16[32,16,1024]{2,1,0:T(8,128)(2,1)}), bf16[32,16,1024]{2,1,0:T(8,128)(2,1)S(1)}, u32[]{:S(2)}, u32[]{:S(2)}) %all-to-all-start.1) | async-done | bytes 1048608 | tf_op jit(solution)/shard_map/all_to_all | solution.py:102
  79.9 3.0 %convolution_select_fusion = f32[512,512]{0,1:T(8,128)} fusion(bf16[512,1024]{1,0:T(8,128)(2,1)S(1)} %bitcast.76, bf16[1024,512]{1,0:T(8,128)(2,1)} %param.18, s32[512]{0:T(512)S(1)} %eq.76, s32[512]{0:T(512)S(1)} %add_select_fusion), kind=kOutput, calls=%fused_computation.7 | convolution fusion | flops 537395200 | bytes 3149824 | tf_op jit(solution)/shard_map/dot_general | solution.py:51
  82.8 1.3 reduce_sum.61
  84.1 14.9 %all-gather = f32[2048,64]{0,1:T(8,128)S(1)} all-gather(f32[512,64]{0,1:T(8,128)S(1)} %reduce_sum.61), channel_id=2, replica_groups=mesh['tp'=4,'ad'=32] {'tp'}, dimensions={0}, use_global_device_ids=true | all-gather | bytes 655360 | tf_op jit(solution)/shard_map/all_gather | solution.py:110
  99.0 0.3 reshape.201
  99.4 0.3 reduce_sum.62
  99.7 1.4 convolution_convert_fusion
  101.1 33.3 %all_to_all.19 = bf16[32,16,2048]{2,1,0:T(8,128)(2,1)} all-to-all(bf16[32,16,2048]{2,1,0:T(8,128)(2,1)S(1)} %bitcast.75), channel_id=1, replica_groups=mesh['tp'=4,'ad'=32] {'ad'}, dimensions={0} | all-to-all | bytes 4194304 | tf_op jit(solution)/shard_map/all_to_all | solution.py:112
  134.4 4.0 %fusion = bf16[256,2048]{1,0:T(8,128)(2,1)} fusion(f32[256,2048]{1,0:T(8,128)} %reduce-scatter.2.cloned.1.call-done, bf16[512,2048]{1,0:T(8,128)(2,1)} %bitcast.70, s32[256]{0:T(256)S(1)} %multiply_add_fusion), kind=kOutput, calls=%fused_computation.2 | convolution fusion | flops 538050560 | bytes 5243904 | tf_op jit(solution)/shard_map/dot_general | solution.py:114
  (31 shorter events, 0.7 us)
Async XLA Ops:
  6.5 93.2 %copy-start = (bf16[512,2048]{1,0:T(8,128)(2,1)S(1)}, bf16[512,2048]{1,0:T(8,128)(2,1)}, u32[]{:S(2)}) copy-start(bf16[512,2048]{1,0:T(8,128)(2,1)} %param.19) | copy-start | bytes 6291460
  6.5 127.9 %reduce-scatter.2.cloned.1.call-start = ((), (), s32[]{:S(2)}) async-start(), calls=%async_computation.4 | async-start | bytes 10485760 | tf_op jit(solution)/shard_map/reduce_scatter | solution.py:116
  7.8 9.2 %copy-start.3 = (bf16[32,8,8,128]{3,2,1,0:T(8,128)(2,1)}, bf16[32,8,8,128]{3,2,1,0:T(8,128)(2,1)S(1)}, u32[]{:S(2)}) copy-start(bf16[32,8,8,128]{3,2,1,0:T(8,128)(2,1)S(1)} %copy.32) | copy-start | bytes 1572868
  10.1 7.0 %copy-start.6 = (bf16[256,128]{1,0:T(8,128)(2,1)S(1)}, bf16[256,128]{1,0:T(8,128)(2,1)}, u32[]{:S(2)}) copy-start(bf16[256,128]{1,0:T(8,128)(2,1)} %param.14) | copy-start | bytes 196612
  26.3 0.8 copy-start.1
  39.5 0.7 copy-start.4
  39.5 0.7 copy-start.5
  39.5 12.1 %copy-start.2 = (bf16[256,8,128]{2,1,0:T(8,128)(2,1)S(1)}, bf16[256,8,128]{2,1,0:T(8,128)(2,1)}, u32[]{:S(2)}) copy-start(bf16[256,8,128]{2,1,0:T(8,128)(2,1)} %copy-done.1) | copy-start | bytes 1572868
  42.2 16.4 %all-to-all-start = ((s32[32,1,16]{2,1,0:T(1,128)}), s32[32,1,16]{2,1,0:T(1,128)S(1)}, u32[]{:S(2)}, u32[]{:S(2)}) async-start(s32[32,1,16]{2,1,0:T(1,128)} %bitcast.4), calls=%async_computation.1 | async-start | bytes 32768 | tf_op jit(solution)/shard_map/all_to_all | solution.py:103
  58.6 21.2 %all-to-all-start.1 = ((bf16[32,16,1024]{2,1,0:T(8,128)(2,1)}), bf16[32,16,1024]{2,1,0:T(8,128)(2,1)S(1)}, u32[]{:S(2)}, u32[]{:S(2)}) async-start(bf16[32,16,1024]{2,1,0:T(8,128)(2,1)} %bitcast.5), calls=%async_computation.2 | async-start | bytes 2097152 | tf_op jit(solution)/shard_map/all_to_all | solution.py:102
Sparse Core Ops, SparseCore 0:
  39.7 87.9 reduce-scatter.1
